TPU v7x, 512 devices: a whole 4x4x16 slice. The times are simulated.
512 devices in a mesh: ctx: 16 (over x, y), exp: 32 (over z, core).
Axes of the slice: x: 4, y: 4, z: 16, core: 2. Of those that a mesh axis runs over, the one named last changes fastest.
Arguments:
- resid: bfloat16 [2048, 3072], P('ctx', 'exp'), may hold values from -37 to 37
- queries: bfloat16 [2048, 4096], P('ctx', 'exp'), may hold values from -6 to 6
- keys: bfloat16 [2048, 4096], P('ctx', 'exp'), may hold values from -0.01171875 to 0.01171875
- values: bfloat16 [2048, 4096], P('ctx', 'exp'), may hold values from -6 to 6
- log_decay: float32 [32, 2048], P('exp', 'ctx'), may hold values from -1.5 to 0
- w_out: bfloat16 [4096, 3072], P('exp'), may hold values from -0.1875 to 0.1875
- w_up: bfloat16 [32, 3072, 6144], P('exp', None, 'ctx'), may hold values from -0.07307089 to 0.07307089
- w_down: bfloat16 [32, 6144, 3072], P('exp', 'ctx'), may hold values from -0.076546554 to 0.076546554
- expert_ids: int32 [2048, 2], P('ctx'), may hold values from 0 to 31, all different within a row; in each aligned block of 128 rows (0 to 127, 128 to 255, ...) at most 16 rows name the same one
- route_weights: float32 [2048, 2], P('ctx'), may hold values from 0.3 to 1.5
- cotangent: bfloat16 [2048, 3072], P('ctx', 'exp'), may hold values from -6 to 6
Outputs:
- layer_out: bfloat16 [2048, 3072], P('ctx', 'exp')
- resid_grad: bfloat16 [2048, 3072], P('ctx', 'exp')
- q_grad: bfloat16 [2048, 4096], P('ctx', 'exp')
- k_grad: bfloat16 [2048, 4096], P('ctx', 'exp')
- v_grad: bfloat16 [2048, 4096], P('ctx', 'exp')
Inputs may be any that keep to these rules, and one draw needn't show every extreme that they name: `expert_ids`: in each aligned block of 128 rows (the positions of one block) no expert is named by more than 16 rows; the two ids of a row differ.
All inputs are finite; a program needn't handle non-finite values.
Results may differ from a plain program's by a relative error of at most 0.02.
Values may be sent and summed in bfloat16 or wider, within the bound.
No kernel may reach another device: no remote copies, remote signals or barrier semaphores. Data moves between devices by JAX's collectives and lax.ppermute only.
A program may use at most 64 MiB of HBM per device.

v0:
```python
import jax
import jax.numpy as jnp
from jax import lax
from jax.sharding import PartitionSpec as P

highest_score = lax.Precision.HIGHEST


def prefix(shard, axis, join, neutral, backward):
    count = lax.axis_size(axis)
    place = lax.axis_index(axis)
    ahead = count - 1 - place if backward else place
    gathered = jax.tree.map(
        lambda a, kind: lax.all_gather(a.astype(kind), axis), shard, (jnp.bfloat16, jnp.bfloat16)
    )
    state = jax.tree.map(lambda a, e: jnp.zeros_like(a) + jnp.asarray(e, a.dtype), shard, neutral)

    def one(hop, state):
        source = count - 1 - hop if backward else hop
        return join(
            state,
            jax.tree.map(
                lambda a, own: lax.dynamic_index_in_dim(a, source, 0, False).astype(own.dtype),
                gathered,
                shard,
            ),
        )

    return lax.fori_loop(0, ahead, one, state)


def block_decays(decay_rows):
    cum = jnp.cumsum(decay_rows, axis=-1)
    last = cum[:, -1]
    token_offset = jnp.arange(decay_rows.shape[-1])
    causal = token_offset[:, None] >= token_offset[None, :]
    gaps = jnp.where(causal[None], cum[:, :, None] - cum[:, None, :], -jnp.inf)
    return (cum, last, jnp.exp(gaps))


def silu_grad(upper):
    sigma = jax.nn.sigmoid(upper)
    return sigma * (1.0 + upper * (1.0 - sigma))


def split_heads(matrix, head_count):
    tokens_here = matrix.shape[0]
    return matrix.astype(jnp.float32).reshape(tokens_here, head_count, -1).transpose(1, 0, 2)


def join_heads(blocks):
    return blocks.transpose(1, 0, 2).reshape(blocks.shape[1], -1).astype(jnp.bfloat16)


def local(
    resid,
    queries,
    keys,
    values,
    log_decay,
    w_out,
    w_up,
    w_down,
    expert_ids,
    route_weights,
    cotangent,
):
    head_count = log_decay.shape[0]
    tokens_here = queries.shape[0]
    query_heads = split_heads(queries, head_count)
    head_keys = split_heads(keys, head_count)
    head_values = split_heads(values, head_count)
    cum, last, decay_matrix = block_decays(log_decay)
    keep_mask = jnp.exp(last[:, None] - cum)[..., None]
    router_scores = (
        jnp.einsum("htd,hid->hti", query_heads, head_keys, precision=highest_score) * decay_matrix
    )
    local_state = jnp.einsum(
        "hid,hie->hde", head_keys * keep_mask, head_values, precision=highest_score
    )

    def link(early, later):
        return (early[0] + later[0], jnp.exp(later[0])[:, None, None] * early[1] + later[1])

    blank = (jnp.zeros_like(last), jnp.zeros_like(local_state))
    _, incoming = prefix((last, local_state), "ctx", link, blank, False)
    inner = jnp.einsum("hti,hid->htd", router_scores, head_values, precision=highest_score)
    outer = jnp.exp(cum)[..., None] * jnp.einsum(
        "htd,hde->hte", query_heads, incoming, precision=highest_score
    )
    attn_heads = join_heads(inner + outer)
    width = w_out.shape[1]
    share = width // lax.axis_size("exp")
    columns = w_out
    attn = (
        lax.psum_scatter(
            lax.dot_general(
                columns, attn_heads, (((0,), (1,)), ((), ())), preferred_element_type=jnp.float32
            ).astype(jnp.bfloat16),
            "exp",
            scatter_dimension=0,
            tiled=True,
        )
        .astype(jnp.float32)
        .T.astype(jnp.bfloat16)
    )
    residual = (resid.astype(jnp.float32) + attn.astype(jnp.float32)).astype(jnp.bfloat16)
    residual_f = residual.astype(jnp.float32)
    square_sum = lax.psum(jnp.sum(residual_f * residual_f, axis=1), "exp")
    rstd = lax.rsqrt(square_sum / width + 1e-06)
    normed = (residual_f * rstd[:, None]).astype(jnp.bfloat16)
    expert_count = w_up.shape[0] * lax.axis_size("exp")
    capacity = 4 * tokens_here // expert_count
    onehot = (expert_ids[:, :, None] == jnp.arange(expert_count)[None, None, :]).astype(jnp.int32)
    flat = onehot.reshape(tokens_here * 2, expert_count)
    before = jnp.cumsum(flat, axis=0) - flat
    slots = jnp.sum(before * flat, axis=1).reshape(tokens_here, 2)
    position = expert_ids * capacity + slots
    place = position[:, :, None] == jnp.arange(expert_count * capacity)[None, None, :]
    picks = place.astype(jnp.bfloat16)
    placed = jnp.sum(place.astype(jnp.int32), axis=1).astype(jnp.bfloat16)
    sent_rows = lax.dot_general(
        placed, normed, (((0,), (0,)), ((), ())), preferred_element_type=jnp.float32
    )
    sent_rows = sent_rows.astype(jnp.bfloat16).reshape(expert_count, capacity, share)
    expert_in = lax.all_to_all(sent_rows, "exp", split_axis=0, concat_axis=2, tiled=True)
    all_rows = lax.all_gather(expert_in, "ctx", axis=1, tiled=True)
    upper = jnp.einsum("erd,edf->erf", all_rows, w_up, preferred_element_type=jnp.float32)
    act = jax.nn.silu(upper).astype(jnp.bfloat16)
    partial_out = jnp.einsum("erf,efd->erd", act, w_down, preferred_element_type=jnp.float32)
    expert_out = lax.psum_scatter(
        partial_out.astype(jnp.bfloat16), "ctx", scatter_dimension=1, tiled=True
    )
    returned = lax.all_to_all(expert_out, "exp", split_axis=2, concat_axis=0, tiled=True).reshape(
        expert_count * capacity, share
    )
    routed = jnp.einsum("tks,sd->tkd", picks, returned, preferred_element_type=jnp.float32)
    layer_out = (residual_f + jnp.sum(route_weights[:, :, None] * routed, axis=1)).astype(
        jnp.bfloat16
    )
    cot_f = cotangent.astype(jnp.float32)
    slot_weight = jnp.einsum(
        "tks,tk->s", place.astype(jnp.float32), route_weights, precision=highest_score
    )
    grad_rows_local = lax.dot_general(
        placed, cotangent, (((0,), (0,)), ((), ())), preferred_element_type=jnp.float32
    )
    grad_send = (
        (grad_rows_local * slot_weight[:, None])
        .astype(jnp.bfloat16)
        .reshape(expert_count, capacity, share)
    )
    grad_in = lax.all_to_all(grad_send, "exp", split_axis=0, concat_axis=2, tiled=True)
    grad_all = lax.all_gather(grad_in, "ctx", axis=1, tiled=True)
    grad_act = jnp.einsum("erd,efd->erf", grad_all, w_down, preferred_element_type=jnp.float32)
    grad_up = (grad_act * silu_grad(upper)).astype(jnp.bfloat16)
    partial_grad = jnp.einsum("erf,edf->erd", grad_up, w_up, preferred_element_type=jnp.float32)
    grad_expert = lax.psum_scatter(
        partial_grad.astype(jnp.bfloat16), "ctx", scatter_dimension=1, tiled=True
    )
    grad_back = lax.all_to_all(grad_expert, "exp", split_axis=2, concat_axis=0, tiled=True).reshape(
        expert_count * capacity, share
    )
    grad_normed = jnp.dot(placed, grad_back, preferred_element_type=jnp.float32)
    inner_dot = lax.psum(jnp.sum(grad_normed * residual_f, axis=1), "exp")
    grad_resid = (
        rstd[:, None] * grad_normed - residual_f * (rstd * rstd * rstd * inner_dot / width)[:, None]
    )
    resid_grad = (cot_f + grad_resid).astype(jnp.bfloat16)
    columns = w_out
    grad_flat = lax.dot_general(
        lax.all_gather(resid_grad, "exp", axis=1, tiled=True),
        columns,
        (((1,), (1,)), ((), ())),
        preferred_element_type=jnp.float32,
    )
    head_gradient = split_heads(grad_flat, head_count)
    local_grad = jnp.einsum(
        "hta,htb->hab",
        query_heads * jnp.exp(cum)[..., None],
        head_gradient,
        precision=highest_score,
    )

    def back_link(early, later):
        return (early[0] + later[0], later[1] + jnp.exp(later[0])[:, None, None] * early[1])

    blank_grad = (jnp.zeros_like(last), jnp.zeros_like(local_grad))
    _, carried_state = prefix((last, local_grad), "ctx", back_link, blank_grad, True)
    score_gradient = (
        jnp.einsum("coy,cwy->cow", head_gradient, head_values, precision=highest_score)
        * decay_matrix
    )
    query_grad = jnp.einsum("hti,hia->hta", score_gradient, head_keys, precision=highest_score)
    query_grad = query_grad + jnp.exp(cum)[..., None] * jnp.einsum(
        "htb,hab->hta", head_gradient, incoming, precision=highest_score
    )
    key_gradient = jnp.einsum("hti,hta->hia", score_gradient, query_heads, precision=highest_score)
    key_gradient = key_gradient + keep_mask * jnp.einsum(
        "qsv,qnv->qsn", head_values, carried_state, precision=highest_score
    )
    value_gradient = jnp.einsum(
        "nyw,nyx->nwx", router_scores, head_gradient, precision=highest_score
    )
    value_gradient = value_gradient + keep_mask * jnp.einsum(
        "sfc,scl->sfl", head_keys, carried_state, precision=highest_score
    )
    return (
        layer_out,
        resid_grad,
        join_heads(query_grad),
        join_heads(key_gradient),
        join_heads(value_gradient),
    )


def solution(mesh):
    return jax.shard_map(
        local,
        mesh=mesh,
        in_specs=(
            P("ctx", "exp"),
            P("ctx", "exp"),
            P("ctx", "exp"),
            P("ctx", "exp"),
            P("exp", "ctx"),
            P("exp", None),
            P("exp", None, "ctx"),
            P("exp", "ctx", None),
            P("ctx", None),
            P("ctx", None),
            P("ctx", "exp"),
        ),
        out_specs=(
            P("ctx", "exp"),
            P("ctx", "exp"),
            P("ctx", "exp"),
            P("ctx", "exp"),
            P("ctx", "exp"),
        ),
        check_vma=False,
    )
```

profile of v0, /device:TPU:32, one launch (start us, length us, event | category | flops | bytes accessed | tf_op | source)
XLA Modules:
  0.0 780.2 jit_solution(4295536002061562439)
XLA Ops:
  13.5 26.2 %all-gather = bf16[2048,128]{1,0:T(8,128)(2,1)} all-gather(bf16[128,128]{1,0:T(8,128)(2,1)S(1)} %convolution_convert_fusion.5), channel_id=2, replica_groups=mesh['ctx'=16,'exp'=32] {'ctx'}, dimensions={0}, use_global_device_ids=true | all-gather | bytes 557056 | tf_op jit(solution)/shard_map/all_gather | solution.py:14
  39.7 38.1 %all-reduce = bf16[16]{0:T(256)(128)(2,1)S(1)} all-reduce(bf16[16]{0:T(256)(128)(2,1)S(1)} %dynamic-update-slice), channel_id=1, replica_groups=mesh['ctx'=16,'exp'=32] {'ctx'}, use_global_device_ids=true, to_apply=%add | all-reduce | flops 16 | bytes 64
  84.2 131.8 %reduce-scatter.10.cloned.1.call-done = bf16[96,128]{1,0:T(8,128)(2,1)} async-done(((bf16[3072,128]{1,0:T(8,128)(2,1)}), bf16[96,128]{1,0:T(8,128)(2,1)}) %reduce-scatter.10.cloned.1.call-update) | async-done | bytes 24592 | tf_op jit(solution)/shard_map/reduce_scatter | solution.py:96
  216.8 45.9 %psum.14 = f32[128]{0:T(128)S(1)} all-reduce(f32[128]{0:T(128)S(1)} %get-tuple-element.215), channel_id=1, replica_groups=mesh['ctx'=16,'exp'=32] {'exp'}, use_global_device_ids=true, to_apply=%region_9.10 | all-reduce | flops 128 | bytes 1024 | tf_op jit(solution)/shard_map/psum | solution.py:109
  263.1 30.3 %all_to_all.66 = bf16[32,16,96]{2,1,0:T(8,128)(2,1)S(1)} all-to-all(bf16[32,16,96]{2,1,0:T(8,128)(2,1)S(1)} %bitcast.175), channel_id=1, replica_groups=mesh['ctx'=16,'exp'=32] {'exp'}, dimensions={0} | all-to-all | bytes 196608 | tf_op jit(solution)/shard_map/all_to_all | solution.py:126
  295.0 20.5 %all_to_all.67 = bf16[32,16,96]{2,1,0:T(8,128)(2,1)S(1)} all-to-all(bf16[32,16,96]{2,1,0:T(8,128)(2,1)S(1)} %bitcast.176), channel_id=1, replica_groups=mesh['ctx'=16,'exp'=32] {'exp'}, dimensions={0} | all-to-all | bytes 196608 | tf_op jit(solution)/shard_map/all_to_all | solution.py:153
  316.4 29.6 %all-gather.5.cloned.1.call-done = bf16[1,256,3072]{2,1,0:T(8,128)(2,1)} async-done(((bf16[1,16,3072]{2,1,0:T(8,128)(2,1)}), bf16[1,256,3072]{2,1,0:T(8,128)(2,1)}) %all-gather.5.cloned.1.call-update) | async-done | bytes 1572880 | tf_op jit(solution)/shard_map/all_gather | solution.py:127
  349.1 59.1 %all-gather.7.cloned.1.call-done = bf16[1,256,3072]{2,1,0:T(8,128)(2,1)} async-done(((bf16[1,16,3072]{2,1,0:T(8,128)(2,1)}), bf16[1,256,3072]{2,1,0:T(8,128)(2,1)}) %all-gather.7.cloned.1.call-update) | async-done | bytes 1572880 | tf_op jit(solution)/shard_map/all_gather | solution.py:154
  408.2 5.2 fusion.1
  415.9 86.2 %reduce-scatter.8.cloned.1.call-done = bf16[1,16,3072]{2,1,0:T(8,128)(2,1)} async-done(((bf16[1,256,3072]{2,1,0:T(8,128)(2,1)}), bf16[1,16,3072]{2,1,0:T(8,128)(2,1)}) %reduce-scatter.8.cloned.1.call-update) | async-done | bytes 98320 | tf_op jit(solution)/shard_map/reduce_scatter | solution.py:158
  502.1 3.6 copy.109
  506.2 18.0 %reduce.2 = bf16[3072,16]{1,0:T(8,128)(2,1)S(1)} reduce(bf16[3072,1,16]{2,1,0:T(2,128)(2,1)} %bitcast.168, bf16[]{:T(256)} %broadcast.70), dimensions={1}, to_apply=%bitcast.130.reduce_sub_computation | reduce | bytes 196610
  525.5 12.9 %all-to-all-start.3 = ((bf16[32,2,768]{2,1,0:T(2,128)(2,1)}), bf16[32,2,768]{2,1,0:T(2,128)(2,1)}, u32[]{:S(2)}, u32[]{:S(2)}) async-start(bf16[32,2,768]{2,1,0:T(2,128)(2,1)} %reshape.274), calls=%async_computation.5 | async-start | bytes 196608 | tf_op jit(solution)/shard_map/all_to_all | solution.py:161
  538.3 56.6 %reduce-scatter.6.cloned.1.call-done = bf16[1,16,3072]{2,1,0:T(8,128)(2,1)} async-done(((bf16[1,256,3072]{2,1,0:T(8,128)(2,1)}), bf16[1,16,3072]{2,1,0:T(8,128)(2,1)}) %reduce-scatter.6.cloned.1.call-update) | async-done | bytes 98320 | tf_op jit(solution)/shard_map/reduce_scatter | solution.py:131
  595.0 3.6 copy.103
  598.6 18.0 %reduce.3 = bf16[3072,16]{1,0:T(8,128)(2,1)S(1)} reduce(bf16[3072,1,16]{2,1,0:T(2,128)(2,1)} %bitcast.169, bf16[]{:T(256)} %broadcast.70), dimensions={1}, to_apply=%bitcast.128.reduce_sub_computation | reduce | bytes 196610
  617.9 12.8 %all-to-all-start.1 = ((bf16[32,2,768]{2,1,0:T(2,128)(2,1)}), bf16[32,2,768]{2,1,0:T(2,128)(2,1)S(1)}, u32[]{:S(2)}, u32[]{:S(2)}) async-start(bf16[32,2,768]{2,1,0:T(2,128)(2,1)} %reshape.272), calls=%async_computation.2 | async-start | bytes 196608 | tf_op jit(solution)/shard_map/all_to_all | solution.py:134
  630.7 4.9 reshape.275
  635.6 3.3 copy.110
  639.4 45.4 %psum.15 = f32[128]{0:T(128)S(1)} all-reduce(f32[128]{0:T(128)S(1)} %get-tuple-element.221), channel_id=1, replica_groups=mesh['ctx'=16,'exp'=32] {'exp'}, use_global_device_ids=true, to_apply=%region_14.15 | all-reduce | flops 128 | bytes 1024 | tf_op jit(solution)/shard_map/psum | solution.py:165
  687.8 3.4 copy.104
  693.9 33.0 %all_gather.32 = bf16[128,3072]{0,1:T(8,128)(2,1)S(1)} all-gather(bf16[128,96]{0,1:T(8,128)(2,1)S(1)} %get-tuple-element.217), channel_id=1, replica_groups=mesh['ctx'=16,'exp'=32] {'exp'}, dimensions={1}, use_global_device_ids=true | all-gather | bytes 811008 | tf_op jit(solution)/shard_map/all_gather | solution.py:172
  728.6 23.3 %all-gather.1 = bf16[2048,128]{1,0:T(8,128)(2,1)S(1)} all-gather(bf16[128,128]{1,0:T(8,128)(2,1)S(1)} %convolution_convert_fusion.4), channel_id=3, replica_groups=mesh['ctx'=16,'exp'=32] {'ctx'}, dimensions={0}, use_global_device_ids=true | all-gather | bytes 557056 | tf_op jit(solution)/shard_map/all_gather | solution.py:14
  751.9 19.2 %while.27 = (s32[]{:T(128)}, f32[1,128,128]{2,1,0:T(8,128)S(1)}, s32[]{:T(128)}, bf16[16,1,128,128]{3,2,1,0:T(8,128)(2,1)S(1)}, bf16[16,1]{0,1:T(2,128)(2,1)S(1)...) while((s32[]{:T(128)}, f32[1,128,128]{2,1,0:T(8,128)S(1)}, s32[]{:T(128)}, ...), condition=%wide.region_16.17_spmd, body=%wide.region_15.16_spmd.sunk | while | flops 49158 | bytes 163997 | solution.py:29
  (154 shorter events, 52.9 us)
Async XLA Ops:
  7.2 401.1 %copy-start = (bf16[1,384,3072]{2,1,0:T(8,128)(2,1)S(1)}, bf16[1,384,3072]{2,1,0:T(8,128)(2,1)}, u32[]{:S(2)}) copy-start(bf16[1,384,3072]{2,1,0:T(8,128)(2,1)} %param.22) | copy-start | bytes 7077892
  7.2 70.7 %copy-start.5 = (bf16[128,128]{1,0:T(8,128)(2,1)S(1)}, bf16[128,128]{1,0:T(8,128)(2,1)}, u32[]{:S(2)}) copy-start(bf16[128,128]{1,0:T(8,128)(2,1)} %param.17) | copy-start | bytes 98308
  7.2 70.9 %copy-start.3 = (bf16[128,128]{1,0:T(8,128)(2,1)S(1)}, bf16[128,128]{1,0:T(8,128)(2,1)}, u32[]{:S(2)}) copy-start(bf16[128,128]{1,0:T(8,128)(2,1)} %param.18) | copy-start | bytes 98308
  7.2 70.7 %copy-start.7 = (bf16[128,128]{1,0:T(8,128)(2,1)S(1)}, bf16[128,128]{1,0:T(8,128)(2,1)}, u32[]{:S(2)}) copy-start(bf16[128,128]{1,0:T(8,128)(2,1)} %param.16) | copy-start | bytes 98308
  7.2 71.6 %copy-start.1 = (bf16[128,3072]{1,0:T(8,128)(2,1)S(1)}, bf16[128,3072]{1,0:T(8,128)(2,1)}, u32[]{:S(2)}) copy-start(bf16[128,3072]{1,0:T(8,128)(2,1)} %param.20) | copy-start | bytes 2359300
  7.2 208.8 %reduce-scatter.10.cloned.1.call-start = ((), (), s32[]{:S(2)}) async-start(), calls=%async_computation.11 | async-start | bytes 811008 | tf_op jit(solution)/shard_map/reduce_scatter | solution.py:96
  8.4 71.8 %copy-start.18 = (f32[1,128]{1,0:T(1,128)}, f32[1,128]{1,0:T(1,128)S(1)}, u32[]{:S(2)}) copy-start(f32[1,128]{1,0:T(1,128)S(1)} %reduce_window_sum.26) | copy-start | bytes 1540
  10.3 67.5 %copy-start.16 = (f32[128]{0:T(128)}, f32[128]{0:T(128)S(1)}, u32[]{:S(2)}) copy-start(f32[128]{0:T(128)S(1)} %get-tuple-element.220) | copy-start | bytes 1540
  10.3 69.8 %copy-start.14 = (f32[128]{0:T(128)}, f32[128]{0:T(128)S(1)}, u32[]{:S(2)}) copy-start(f32[128]{0:T(128)S(1)} %get-tuple-element.219) | copy-start | bytes 1540
  80.1 135.9 %copy-start.13 = (bf16[128,96]{0,1:T(8,128)(2,1)S(1)}, bf16[128,96]{0,1:T(8,128)(2,1)}, u32[]{:S(2)}) copy-start(bf16[128,96]{0,1:T(8,128)(2,1)} %param.15) | copy-start | bytes 73732
  82.5 211.9 %copy-start.22 = (f32[128,2]{0,1:T(2,128)S(1)}, f32[128,2]{0,1:T(2,128)}, u32[]{:S(2)}) copy-start(f32[128,2]{0,1:T(2,128)} %param.24) | copy-start | bytes 3076
  82.5 212.2 %copy-start.12 = (bf16[128,96]{0,1:T(8,128)(2,1)S(1)}, bf16[128,96]{0,1:T(8,128)(2,1)}, u32[]{:S(2)}) copy-start(bf16[128,96]{0,1:T(8,128)(2,1)} %param.25) | copy-start | bytes 73732
  82.5 263.5 %all-gather.5.cloned.1.call-start = ((), (), s32[]{:S(2)}) async-start(), calls=%async_computation.7 | async-start | bytes 1671168 | tf_op jit(solution)/shard_map/all_gather | solution.py:127
  294.3 113.9 %all-gather.7.cloned.1.call-start = ((), (), s32[]{:S(2)}) async-start(), calls=%async_computation.9 | async-start | bytes 1671168 | tf_op jit(solution)/shard_map/all_gather | solution.py:154
  316.4 185.7 %reduce-scatter.8.cloned.1.call-start = ((), (), s32[]{:S(2)}) async-start(), calls=%async_computation.10 | async-start | bytes 1671168 | tf_op jit(solution)/shard_map/reduce_scatter | solution.py:158
  413.5 181.5 %reduce-scatter.6.cloned.1.call-start = ((), (), s32[]{:S(2)}) async-start(), calls=%async_computation.8 | async-start | bytes 1671168 | tf_op jit(solution)/shard_map/reduce_scatter | solution.py:131
  525.5 92.4 %all-to-all-start.3 = ((bf16[32,2,768]{2,1,0:T(2,128)(2,1)}), bf16[32,2,768]{2,1,0:T(2,128)(2,1)}, u32[]{:S(2)}, u32[]{:S(2)}) async-start(bf16[32,2,768]{2,1,0:T(2,128)(2,1)} %reshape.274), calls=%async_computation.5 | async-start | bytes 196608 | tf_op jit(solution)/shard_map/all_to_all | solution.py:161
  617.9 67.5 %all-to-all-start.1 = ((bf16[32,2,768]{2,1,0:T(2,128)(2,1)}), bf16[32,2,768]{2,1,0:T(2,128)(2,1)S(1)}, u32[]{:S(2)}, u32[]{:S(2)}) async-start(bf16[32,2,768]{2,1,0:T(2,128)(2,1)} %reshape.272), calls=%async_computation.2 | async-start | bytes 196608 | tf_op jit(solution)/shard_map/all_to_all | solution.py:134
  687.7 39.1 %copy-start.2 = (bf16[128,3072]{1,0:T(8,128)(2,1)S(1)}, bf16[128,3072]{1,0:T(8,128)(2,1)}, u32[]{:S(2)}) copy-start(bf16[128,3072]{1,0:T(8,128)(2,1)} %param.20) | copy-start | bytes 2359300
  691.3 35.9 %copy-start.8 = (bf16[128,128]{1,0:T(8,128)(2,1)S(1)}, bf16[128,128]{1,0:T(8,128)(2,1)}, u32[]{:S(2)}) copy-start(bf16[128,128]{1,0:T(8,128)(2,1)} %param.16) | copy-start | bytes 98308
  691.4 36.2 %copy-start.10 = (f32[128,128]{1,0:T(8,128)S(1)}, f32[128,128]{1,0:T(8,128)}, u32[]{:S(2)}) copy-start(f32[128,128]{1,0:T(8,128)} %copy-done.9) | copy-start | bytes 196612
  691.4 36.5 %copy-start.4 = (bf16[128,128]{1,0:T(8,128)(2,1)S(1)}, bf16[128,128]{1,0:T(8,128)(2,1)}, u32[]{:S(2)}) copy-start(bf16[128,128]{1,0:T(8,128)(2,1)} %param.18) | copy-start | bytes 98308
  691.4 36.5 %copy-start.19 = (f32[1,128]{1,0:T(1,128)S(1)}, f32[1,128]{1,0:T(1,128)}, u32[]{:S(2)}) copy-start(f32[1,128]{1,0:T(1,128)} %copy-done.18) | copy-start | bytes 1540
  727.3 43.9 %copy-start.17 = (f32[128]{0:T(128)S(1)}, f32[128]{0:T(128)}, u32[]{:S(2)}) copy-start(f32[128]{0:T(128)} %copy-done.16) | copy-start | bytes 1540
  (8 other events, 169.5 us)
Sparse Core Ops, SparseCore 0:
  82.6 133.4 reduce-scatter.9
  294.4 51.4 all-gather.4
  349.5 58.7 all-gather.6
  413.6 88.4 reduce-scatter.7
  506.6 88.3 reduce-scatter.5
where the time goes:
time: 783 us; the launch traced here: 780 us
  waiting for transfers between devices  363 us (46%)
  blocking collectives  263 us (34%)
  other arithmetic  51.2 us (7%)
  local copies, waits for them, and re-layouts  41.8 us (5%)
  starting transfers between devices  26.1 us (3%)
  matrix products  19.5 us (2%)
  between operations  15 us (2%)
    reduce_scatter x1, waiting for transfers between devices, local(): lax.psum_scatter(lax.dot_general(columns, attn_heads, (((0,), (1,)), ((),...  132 us
    reduce_scatter x1, waiting for transfers between devices, local(): lax.psum_scatter(partial_grad.astype(jnp.bfloat16), 'ctx', scatter_dimens...  86.2 us
    all_gather x1, waiting for transfers between devices, local(): grad_all = lax.all_gather(grad_in, 'ctx', axis=1, tiled=True)  59.1 us
    reduce_scatter x1, waiting for transfers between devices, local(): lax.psum_scatter(partial_out.astype(jnp.bfloat16), 'ctx', scatter_dimensi...  56.6 us
    all_gather x2, blocking collectives, prefix(): lax.all_gather(a.astype(kind), axis)  49.5 us
    psum x1, blocking collectives, local(): square_sum = lax.psum(jnp.sum(residual_f * residual_f, axis=1), 'exp')  45.9 us
    psum x1, blocking collectives, local(): inner_dot = lax.psum(jnp.sum(grad_normed * residual_f, axis=1), 'exp')  45.4 us
    unnamed x1, blocking collectives  38.1 us
  transfers between devices with their start and end apart: 7, of which 5 were waited for; matrix products, arithmetic and copies ran while one was open for 8% of the time, Pallas kernels for 0%

commit v1 on v0

--- a/solution.py
+++ b/solution.py
@@ -4,6 +4,19 @@
 from jax.sharding import PartitionSpec as P
 
 highest_score = lax.Precision.HIGHEST
+
+
+def ring_gather(shard, axis, dim):
+    ways = lax.axis_size(axis)
+    up = [(d, (d + 1) % ways) for d in range(ways)]
+    down = [(d, (d - 1) % ways) for d in range(ways)]
+    earlier, later = ([shard], [shard])
+    for _ in range(ways // 2):
+        earlier.append(lax.ppermute(earlier[-1], axis, up))
+    for _ in range((ways - 1) // 2):
+        later.append(lax.ppermute(later[-1], axis, down))
+    line = jnp.concatenate([*earlier[::-1], *later[1:]], axis=dim)
+    return jnp.roll(line, (lax.axis_index(axis) - ways // 2) * shard.shape[dim], axis=dim)
 
 
 def prefix(shard, axis, join, neutral, backward):
@@ -151,7 +164,7 @@
         .reshape(expert_count, capacity, share)
     )
     grad_in = lax.all_to_all(grad_send, "exp", split_axis=0, concat_axis=2, tiled=True)
-    grad_all = lax.all_gather(grad_in, "ctx", axis=1, tiled=True)
+    grad_all = ring_gather(grad_in, "ctx", 1)
     grad_act = jnp.einsum("erd,efd->erf", grad_all, w_down, preferred_element_type=jnp.float32)
     grad_up = (grad_act * silu_grad(upper)).astype(jnp.bfloat16)
     partial_grad = jnp.einsum("erf,edf->erd", grad_up, w_up, preferred_element_type=jnp.float32)

time: 783 us -> 848 us (1.083)
  starting transfers between devices: 26.1 us -> 157 us
  waiting for transfers between devices: 363 us -> 276 us
  local copies, waits for them, and re-layouts: 41.8 us -> 105 us
  blocking collectives: 263 us -> 214 us
    ppermute x0 -> x15, starting transfers between devices: none -> 100 us  [the longest x7 81.2 us: ring_gather(): later.append(lax.ppermute(later[-1], axis, down))]
    reduce_scatter x1, waiting for transfers between devices: 132 us -> 61 us  [local(): lax.psum_scatter(lax.dot_general(columns, attn_heads, (((0,), (1,)), ((),...]
    all_gather x1 -> x0, waiting for transfers between devices: 59.1 us -> none  [local(): grad_all = lax.all_gather(grad_in, 'ctx', axis=1, tiled=True)]
    all_to_all x2 -> x0, blocking collectives: 50.8 us -> none  [the longest x1 30.3 us: local(): lax.all_to_all(sent_rows, 'exp', split_axis=0, concat_axis=2, tiled=True)]
    unnamed x60 -> x83, local copies, waits for them, and re-layouts: 15.4 us -> 61.4 us
    all_to_all x0 -> x2, starting transfers between devices: none -> 30.1 us  [the longest x1 15.4 us: local(): lax.all_to_all(grad_send, 'exp', split_axis=0, concat_axis=2, tiled=True)]
    all_to_all x0 -> x2, waiting for transfers between devices: none -> 26.8 us  [the longest x1 14.1 us: local(): lax.all_to_all(grad_send, 'exp', split_axis=0, concat_axis=2, tiled=True)]
    all_gather x1, waiting for transfers between devices: 29.6 us -> 41.4 us  [local(): all_rows = lax.all_gather(expert_in, 'ctx', axis=1, tiled=True)]
  transfers between devices with their start and end apart: 7 -> 23, of which waited for: 5 -> 8; matrix products, arithmetic and copies ran while one was open for 8% -> 13% of each run, Pallas kernels for 0% -> 0%
where the time goes in v1:
time: 848 us; the launch traced here: 843 us
  waiting for transfers between devices  276 us (33%)
  blocking collectives  214 us (25%)
  starting transfers between devices  157 us (19%)
  local copies, waits for them, and re-layouts  105 us (12%)
  other arithmetic  50.9 us (6%)
  matrix products  25.3 us (3%)
  between operations  15.1 us (2%)
    reduce_scatter x1, waiting for transfers between devices, local(): lax.psum_scatter(partial_grad.astype(jnp.bfloat16), 'ctx', scatter_dimens...  86.2 us
    ppermute x7, starting transfers between devices, ring_gather(): later.append(lax.ppermute(later[-1], axis, down))  81.2 us
    unnamed x83, local copies, waits for them, and re-layouts  61.4 us
    reduce_scatter x1, waiting for transfers between devices, local(): lax.psum_scatter(lax.dot_general(columns, attn_heads, (((0,), (1,)), ((),...  61 us
    reduce_scatter x1, waiting for transfers between devices, local(): lax.psum_scatter(partial_out.astype(jnp.bfloat16), 'ctx', scatter_dimensi...  56.6 us
    all_gather x2, blocking collectives, prefix(): lax.all_gather(a.astype(kind), axis)  48.1 us
    psum x1, blocking collectives, local(): square_sum = lax.psum(jnp.sum(residual_f * residual_f, axis=1), 'exp')  46 us
    psum x1, blocking collectives, local(): inner_dot = lax.psum(jnp.sum(grad_normed * residual_f, axis=1), 'exp')  45.4 us
  transfers between devices with their start and end apart: 23, of which 8 were waited for; matrix products, arithmetic and copies ran while one was open for 13% of the time, Pallas kernels for 0%

profile of v1, /device:TPU:32, one launch (start us, length us, event | category | flops | bytes accessed | tf_op | source)
XLA Modules:
  0.0 842.8 jit_solution(4550719454274173673)
XLA Ops:
  13.1 15.4 %all-to-all-start.2 = ((bf16[32,16,96]{2,1,0:T(8,128)(2,1)}), bf16[32,16,96]{2,1,0:T(8,128)(2,1)S(1)}, u32[]{:S(2)}, u32[]{:S(2)}) async-start(bf16[32,16,96]{2,1,0:T(8,128)(2,1)} %bitcast.29), calls=%async_computation.3 | async-start | bytes 262144 | tf_op jit(solution)/shard_map/all_to_all | solution.py:166
  30.0 14.1 %all-to-all-done.2 = bf16[32,16,96]{2,1,0:T(8,128)(2,1)S(1)} async-done(((bf16[32,16,96]{2,1,0:T(8,128)(2,1)}), bf16[32,16,96]{2,1,0:T(8,128)(2,1)S(1)}, u32[]{:S(2)}, u32[]{:S(2)}) %all-to-all-start.2) | async-done | bytes 98336 | tf_op jit(solution)/shard_map/all_to_all | solution.py:166
  58.9 41.5 %all-reduce = bf16[16]{0:T(256)(128)(2,1)} all-reduce(bf16[16]{0:T(256)(128)(2,1)} %copy-done.20), channel_id=1, replica_groups=mesh['ctx'=16,'exp'=32] {'ctx'}, use_global_device_ids=true, to_apply=%add | all-reduce | flops 16 | bytes 64
  106.2 24.8 %all-gather = bf16[2048,128]{1,0:T(8,128)(2,1)} all-gather(bf16[128,128]{1,0:T(8,128)(2,1)S(1)} %convolution_convert_fusion.5), channel_id=2, replica_groups=mesh['ctx'=16,'exp'=32] {'ctx'}, dimensions={0}, use_global_device_ids=true | all-gather | bytes 557056 | tf_op jit(solution)/shard_map/all_gather | solution.py:27
  138.3 46.4 %collective-permute-start.10 = (bf16[1,16,3072]{2,1,0:T(8,128)(2,1)}, bf16[1,16,3072]{2,1,0:T(8,128)(2,1)S(1)}, u32[]{:S(2)}, u32[]{:S(2)}) collective-permute-start(bf16[1,16,3072]{2,1,0:T(8,128)(2,1)} %collective-permute-done.9), channel_id=1, source_target_pairs={{0,480},{32,0},{64,32},{96,64},{128,96},{160,128},{192,160},{224,1... | collective-permute-start | bytes 294920 | tf_op jit(solution)/shard_map/ppermute | solution.py:17
  188.2 7.2 collective-permute-start.11
  199.0 7.2 collective-permute-start.12
  209.1 7.2 collective-permute-start.13
  222.0 7.2 collective-permute-start.14
  258.0 61.0 %reduce-scatter.10.cloned.1.call-done = bf16[96,128]{1,0:T(8,128)(2,1)} async-done(((bf16[3072,128]{1,0:T(8,128)(2,1)}), bf16[96,128]{1,0:T(8,128)(2,1)}) %reduce-scatter.10.cloned.1.call-update) | async-done | bytes 24592 | tf_op jit(solution)/shard_map/reduce_scatter | solution.py:109
  319.7 46.0 %psum.14 = f32[128]{0:T(128)S(1)} all-reduce(f32[128]{0:T(128)S(1)} %get-tuple-element.215), channel_id=1, replica_groups=mesh['ctx'=16,'exp'=32] {'exp'}, use_global_device_ids=true, to_apply=%region_9.10 | all-reduce | flops 128 | bytes 1024 | tf_op jit(solution)/shard_map/psum | solution.py:122
  366.6 14.7 %all-to-all-start = ((bf16[32,16,96]{2,1,0:T(8,128)(2,1)}), bf16[32,16,96]{2,1,0:T(8,128)(2,1)S(1)}, u32[]{:S(2)}, u32[]{:S(2)}) async-start(bf16[32,16,96]{2,1,0:T(8,128)(2,1)} %bitcast.16), calls=%async_computation | async-start | bytes 262144 | tf_op jit(solution)/shard_map/all_to_all | solution.py:139
  384.5 12.6 %all-to-all-done = bf16[32,16,96]{2,1,0:T(8,128)(2,1)S(1)} async-done(((bf16[32,16,96]{2,1,0:T(8,128)(2,1)}), bf16[32,16,96]{2,1,0:T(8,128)(2,1)S(1)}, u32[]{:S(2)}, u32[]{:S(2)}) %all-to-all-start) | async-done | bytes 98336 | tf_op jit(solution)/shard_map/all_to_all | solution.py:139
  408.2 41.4 %all-gather.4.cloned.1.call-done = bf16[1,256,3072]{2,1,0:T(8,128)(2,1)} async-done(((bf16[1,16,3072]{2,1,0:T(8,128)(2,1)}), bf16[1,256,3072]{2,1,0:T(8,128)(2,1)}) %all-gather.4.cloned.1.call-update) | async-done | bytes 1572880 | tf_op jit(solution)/shard_map/all_gather | solution.py:140
  460.4 86.2 %reduce-scatter.8.cloned.1.call-done = bf16[1,16,3072]{2,1,0:T(8,128)(2,1)} async-done(((bf16[1,256,3072]{2,1,0:T(8,128)(2,1)}), bf16[1,16,3072]{2,1,0:T(8,128)(2,1)}) %reduce-scatter.8.cloned.1.call-update) | async-done | bytes 98320 | tf_op jit(solution)/shard_map/reduce_scatter | solution.py:171
  550.8 18.0 %reduce.2 = bf16[3072,16]{1,0:T(8,128)(2,1)S(1)} reduce(bf16[3072,1,16]{2,1,0:T(2,128)(2,1)} %bitcast.168, bf16[]{:T(256)} %broadcast.71), dimensions={1}, to_apply=%bitcast.130.reduce_sub_computation | reduce | bytes 196610
  570.1 12.9 %all-to-all-start.3 = ((bf16[32,2,768]{2,1,0:T(2,128)(2,1)}), bf16[32,2,768]{2,1,0:T(2,128)(2,1)}, u32[]{:S(2)}, u32[]{:S(2)}) async-start(bf16[32,2,768]{2,1,0:T(2,128)(2,1)} %reshape.274), calls=%async_computation.5 | async-start | bytes 196608 | tf_op jit(solution)/shard_map/all_to_all | solution.py:174
  583.0 56.6 %reduce-scatter.6.cloned.1.call-done = bf16[1,16,3072]{2,1,0:T(8,128)(2,1)} async-done(((bf16[1,256,3072]{2,1,0:T(8,128)(2,1)}), bf16[1,16,3072]{2,1,0:T(8,128)(2,1)}) %reduce-scatter.6.cloned.1.call-update) | async-done | bytes 98320 | tf_op jit(solution)/shard_map/reduce_scatter | solution.py:144
  643.2 18.0 %reduce.3 = bf16[3072,16]{1,0:T(8,128)(2,1)S(1)} reduce(bf16[3072,1,16]{2,1,0:T(2,128)(2,1)} %bitcast.169, bf16[]{:T(256)} %broadcast.71), dimensions={1}, to_apply=%bitcast.128.reduce_sub_computation | reduce | bytes 196610
  662.4 12.9 %all-to-all-start.1 = ((bf16[32,2,768]{2,1,0:T(2,128)(2,1)}), bf16[32,2,768]{2,1,0:T(2,128)(2,1)}, u32[]{:S(2)}, u32[]{:S(2)}) async-start(bf16[32,2,768]{2,1,0:T(2,128)(2,1)} %reshape.272), calls=%async_computation.2 | async-start | bytes 196608 | tf_op jit(solution)/shard_map/all_to_all | solution.py:147
  687.7 45.4 %psum.15 = f32[128]{0:T(128)S(1)} all-reduce(f32[128]{0:T(128)S(1)} %get-tuple-element.221), channel_id=1, replica_groups=mesh['ctx'=16,'exp'=32] {'exp'}, use_global_device_ids=true, to_apply=%region_14.15 | all-reduce | flops 128 | bytes 1024 | tf_op jit(solution)/shard_map/psum | solution.py:178
  744.7 32.9 %all_gather.28 = bf16[128,3072]{0,1:T(8,128)(2,1)S(1)} all-gather(bf16[128,96]{0,1:T(8,128)(2,1)S(1)} %get-tuple-element.217), channel_id=1, replica_groups=mesh['ctx'=16,'exp'=32] {'exp'}, dimensions={1}, use_global_device_ids=true | all-gather | bytes 811008 | tf_op jit(solution)/shard_map/all_gather | solution.py:185
  779.3 23.3 %all-gather.1 = bf16[2048,128]{1,0:T(8,128)(2,1)S(1)} all-gather(bf16[128,128]{1,0:T(8,128)(2,1)S(1)} %convolution_convert_fusion.4), channel_id=3, replica_groups=mesh['ctx'=16,'exp'=32] {'ctx'}, dimensions={0}, use_global_device_ids=true | all-gather | bytes 557056 | tf_op jit(solution)/shard_map/all_gather | solution.py:27
  802.6 29.6 %while.27 = (s32[]{:T(128)}, f32[1,128,128]{2,1,0:T(8,128)S(1)}, s32[]{:T(128)}, bf16[16,1,128,128]{3,2,1,0:T(8,128)(2,1)S(1)}, bf16[16,1]{0,1:T(2,128)(2,1)}, /*index=5*/s32[]{:T(128)}, s32[]{:T(128)}, s32[]{:T(128)}, s32[]{:T(128)}) while((s32[]{:T(128)}, f32[1,128,128]{2,1,0:T(8,128)S(1)}, s32[]{:T(128)}, ...), condition=%wide.region_16.17_spmd, body=%wide.region_15.16_spmd.sunk | while | flops 49158 | bytes 163997 | solution.py:42
  (207 shorter events, 174.3 us)
Async XLA Ops:
  7.2 445.6 %copy-start = (bf16[1,384,3072]{2,1,0:T(8,128)(2,1)S(1)}, bf16[1,384,3072]{2,1,0:T(8,128)(2,1)}, u32[]{:S(2)}) copy-start(bf16[1,384,3072]{2,1,0:T(8,128)(2,1)} %param.22) | copy-start | bytes 7077892
  13.1 31.1 %all-to-all-start.2 = ((bf16[32,16,96]{2,1,0:T(8,128)(2,1)}), bf16[32,16,96]{2,1,0:T(8,128)(2,1)S(1)}, u32[]{:S(2)}, u32[]{:S(2)}) async-start(bf16[32,16,96]{2,1,0:T(8,128)(2,1)} %bitcast.29), calls=%async_computation.3 | async-start | bytes 262144 | tf_op jit(solution)/shard_map/all_to_all | solution.py:166
  28.4 290.5 %reduce-scatter.10.cloned.1.call-start = ((), (), s32[]{:S(2)}) async-start(), calls=%async_computation.10 | async-start | bytes 811008 | tf_op jit(solution)/shard_map/reduce_scatter | solution.py:109
  45.9 9.9 %collective-permute-start = (bf16[1,16,3072]{2,1,0:T(8,128)(2,1)S(1)}, bf16[1,16,3072]{2,1,0:T(8,128)(2,1)}, u32[]{:S(2)}, u32[]{:S(2)}) collective-permute-start(bf16[1,16,3072]{2,1,0:T(8,128)(2,1)S(1)} %all_to_all.58), channel_id=1, source_target_pairs={{0,32},{32,64},{64,96},{96,128},{128,160},{160,192},{192,224},{224... | collective-permute-start | bytes 294920 | tf_op jit(solution)/shard_map/ppermute | solution.py:15
  55.9 46.4 %collective-permute-start.1 = (bf16[1,16,3072]{2,1,0:T(8,128)(2,1)}, bf16[1,16,3072]{2,1,0:T(8,128)(2,1)}, u32[]{:S(2)}, u32[]{:S(2)}) collective-permute-start(bf16[1,16,3072]{2,1,0:T(8,128)(2,1)} %collective-permute-done), channel_id=1, source_target_pairs={{0,32},{32,64},{64,96},{96,128},{128,160},{160,192},{192,224},{224... | collective-permute-start | bytes 294920 | tf_op jit(solution)/shard_map/ppermute | solution.py:15
  100.4 30.7 %collective-permute-start.8 = (bf16[1,16,3072]{2,1,0:T(8,128)(2,1)S(1)}, bf16[1,16,3072]{2,1,0:T(8,128)(2,1)}, u32[]{:S(2)}, u32[]{:S(2)}) collective-permute-start(bf16[1,16,3072]{2,1,0:T(8,128)(2,1)S(1)} %all_to_all.58), channel_id=1, source_target_pairs={{0,480},{32,0},{64,32},{96,64},{128,96},{160,128},{192,160},{224,1... | collective-permute-start | bytes 294920 | tf_op jit(solution)/shard_map/ppermute | solution.py:17
  102.3 32.7 %collective-permute-start.2 = (bf16[1,16,3072]{2,1,0:T(8,128)(2,1)}, bf16[1,16,3072]{2,1,0:T(8,128)(2,1)}, u32[]{:S(2)}, u32[]{:S(2)}) collective-permute-start(bf16[1,16,3072]{2,1,0:T(8,128)(2,1)} %collective-permute-done.1), channel_id=1, source_target_pairs={{0,32},{32,64},{64,96},{96,128},{128,160},{160,192},{192,224},{224... | collective-permute-start | bytes 294920 | tf_op jit(solution)/shard_map/ppermute | solution.py:15
  131.1 7.2 collective-permute-start.9
  135.0 49.6 %collective-permute-start.3 = (bf16[1,16,3072]{2,1,0:T(8,128)(2,1)}, bf16[1,16,3072]{2,1,0:T(8,128)(2,1)}, u32[]{:S(2)}, u32[]{:S(2)}) collective-permute-start(bf16[1,16,3072]{2,1,0:T(8,128)(2,1)} %collective-permute-done.2), channel_id=1, source_target_pairs={{0,32},{32,64},{64,96},{96,128},{128,160},{160,192},{192,224},{224... | collective-permute-start | bytes 294920 | tf_op jit(solution)/shard_map/ppermute | solution.py:15
  138.3 49.3 %collective-permute-start.10 = (bf16[1,16,3072]{2,1,0:T(8,128)(2,1)}, bf16[1,16,3072]{2,1,0:T(8,128)(2,1)S(1)}, u32[]{:S(2)}, u32[]{:S(2)}) collective-permute-start(bf16[1,16,3072]{2,1,0:T(8,128)(2,1)} %collective-permute-done.9), channel_id=1, source_target_pairs={{0,480},{32,0},{64,32},{96,64},{128,96},{160,128},{192,160},{224,1... | collective-permute-start | bytes 294920 | tf_op jit(solution)/shard_map/ppermute | solution.py:17
  184.7 10.8 %collective-permute-start.4 = (bf16[1,16,3072]{2,1,0:T(8,128)(2,1)}, bf16[1,16,3072]{2,1,0:T(8,128)(2,1)S(1)}, u32[]{:S(2)}, u32[]{:S(2)}) collective-permute-start(bf16[1,16,3072]{2,1,0:T(8,128)(2,1)} %collective-permute-done.3), channel_id=1, source_target_pairs={{0,32},{32,64},{64,96},{96,128},{128,160},{160,192},{192,224},{224... | collective-permute-start | bytes 294920 | tf_op jit(solution)/shard_map/ppermute | solution.py:15
  188.2 10.1 %collective-permute-start.11 = (bf16[1,16,3072]{2,1,0:T(8,128)(2,1)S(1)}, bf16[1,16,3072]{2,1,0:T(8,128)(2,1)S(1)}, u32[]{:S(2)}, u32[]{:S(2)}) collective-permute-start(bf16[1,16,3072]{2,1,0:T(8,128)(2,1)S(1)} %collective-permute-done.10), channel_id=1, source_target_pairs={{0,480},{32,0},{64,32},{96,64},{128,96},{160,128},{192,160},{224,1... | collective-permute-start | bytes 294920 | tf_op jit(solution)/shard_map/ppermute | solution.py:17
  195.5 10.8 %collective-permute-start.5 = (bf16[1,16,3072]{2,1,0:T(8,128)(2,1)S(1)}, bf16[1,16,3072]{2,1,0:T(8,128)(2,1)S(1)}, u32[]{:S(2)}, u32[]{:S(2)}) collective-permute-start(bf16[1,16,3072]{2,1,0:T(8,128)(2,1)S(1)} %collective-permute-done.4), channel_id=1, source_target_pairs={{0,32},{32,64},{64,96},{96,128},{128,160},{160,192},{192,224},{224... | collective-permute-start | bytes 294920 | tf_op jit(solution)/shard_map/ppermute | solution.py:15
  199.0 10.1 %collective-permute-start.12 = (bf16[1,16,3072]{2,1,0:T(8,128)(2,1)S(1)}, bf16[1,16,3072]{2,1,0:T(8,128)(2,1)}, u32[]{:S(2)}, u32[]{:S(2)}) collective-permute-start(bf16[1,16,3072]{2,1,0:T(8,128)(2,1)S(1)} %collective-permute-done.11), channel_id=1, source_target_pairs={{0,480},{32,0},{64,32},{96,64},{128,96},{160,128},{192,160},{224,1... | collective-permute-start | bytes 294920 | tf_op jit(solution)/shard_map/ppermute | solution.py:17
  206.2 10.2 %collective-permute-start.6 = (bf16[1,16,3072]{2,1,0:T(8,128)(2,1)S(1)}, bf16[1,16,3072]{2,1,0:T(8,128)(2,1)}, u32[]{:S(2)}, u32[]{:S(2)}) collective-permute-start(bf16[1,16,3072]{2,1,0:T(8,128)(2,1)S(1)} %collective-permute-done.5), channel_id=1, source_target_pairs={{0,32},{32,64},{64,96},{96,128},{128,160},{160,192},{192,224},{224... | collective-permute-start | bytes 294920 | tf_op jit(solution)/shard_map/ppermute | solution.py:15
  209.1 12.9 %collective-permute-start.13 = (bf16[1,16,3072]{2,1,0:T(8,128)(2,1)}, bf16[1,16,3072]{2,1,0:T(8,128)(2,1)}, u32[]{:S(2)}, u32[]{:S(2)}) collective-permute-start(bf16[1,16,3072]{2,1,0:T(8,128)(2,1)} %collective-permute-done.12), channel_id=1, source_target_pairs={{0,480},{32,0},{64,32},{96,64},{128,96},{160,128},{192,160},{224,1... | collective-permute-start | bytes 294920 | tf_op jit(solution)/shard_map/ppermute | solution.py:17
  216.4 12.9 %collective-permute-start.7 = (bf16[1,16,3072]{2,1,0:T(8,128)(2,1)}, bf16[1,16,3072]{2,1,0:T(8,128)(2,1)}, u32[]{:S(2)}, u32[]{:S(2)}) collective-permute-start(bf16[1,16,3072]{2,1,0:T(8,128)(2,1)} %collective-permute-done.6), channel_id=1, source_target_pairs={{0,32},{32,64},{64,96},{96,128},{128,160},{160,192},{192,224},{224... | collective-permute-start | bytes 294920 | tf_op jit(solution)/shard_map/ppermute | solution.py:15
  222.0 29.4 %collective-permute-start.14 = (bf16[1,16,3072]{2,1,0:T(8,128)(2,1)}, bf16[1,16,3072]{2,1,0:T(8,128)(2,1)S(1)}, u32[]{:S(2)}, u32[]{:S(2)}) collective-permute-start(bf16[1,16,3072]{2,1,0:T(8,128)(2,1)} %collective-permute-done.13), channel_id=1, source_target_pairs={{0,480},{32,0},{64,32},{96,64},{128,96},{160,128},{192,160},{224,1... | collective-permute-start | bytes 294920 | tf_op jit(solution)/shard_map/ppermute | solution.py:17
  366.6 30.5 %all-to-all-start = ((bf16[32,16,96]{2,1,0:T(8,128)(2,1)}), bf16[32,16,96]{2,1,0:T(8,128)(2,1)S(1)}, u32[]{:S(2)}, u32[]{:S(2)}) async-start(bf16[32,16,96]{2,1,0:T(8,128)(2,1)} %bitcast.16), calls=%async_computation | async-start | bytes 262144 | tf_op jit(solution)/shard_map/all_to_all | solution.py:139
  381.4 68.3 %all-gather.4.cloned.1.call-start = ((), (), s32[]{:S(2)}) async-start(), calls=%async_computation.7 | async-start | bytes 1671168 | tf_op jit(solution)/shard_map/all_gather | solution.py:140
  398.0 148.7 %reduce-scatter.8.cloned.1.call-start = ((), (), s32[]{:S(2)}) async-start(), calls=%async_computation.9 | async-start | bytes 1671168 | tf_op jit(solution)/shard_map/reduce_scatter | solution.py:171
  458.0 181.5 %reduce-scatter.6.cloned.1.call-start = ((), (), s32[]{:S(2)}) async-start(), calls=%async_computation.8 | async-start | bytes 1671168 | tf_op jit(solution)/shard_map/reduce_scatter | solution.py:144
  570.1 92.4 %all-to-all-start.3 = ((bf16[32,2,768]{2,1,0:T(2,128)(2,1)}), bf16[32,2,768]{2,1,0:T(2,128)(2,1)}, u32[]{:S(2)}, u32[]{:S(2)}) async-start(bf16[32,2,768]{2,1,0:T(2,128)(2,1)} %reshape.274), calls=%async_computation.5 | async-start | bytes 196608 | tf_op jit(solution)/shard_map/all_to_all | solution.py:174
  662.4 70.7 %all-to-all-start.1 = ((bf16[32,2,768]{2,1,0:T(2,128)(2,1)}), bf16[32,2,768]{2,1,0:T(2,128)(2,1)}, u32[]{:S(2)}, u32[]{:S(2)}) async-start(bf16[32,2,768]{2,1,0:T(2,128)(2,1)} %reshape.272), calls=%async_computation.2 | async-start | bytes 196608 | tf_op jit(solution)/shard_map/all_to_all | solution.py:147
  (20 other events, 1141.3 us)
Sparse Core Ops, SparseCore 0:
  222.1 96.8 reduce-scatter.9
  398.1 51.5 all-gather.3
  458.1 88.4 reduce-scatter.7
  551.1 88.3 reduce-scatter.5
